TPU v7x, 32 devices: a whole 2x2x4 slice. The times are simulated.
32 devices in a mesh: lon: 16 (over z, x, core), lat: 2 (over y).
Axes of the slice: x: 2, y: 2, z: 4, core: 2. Of those that a mesh axis runs over, the one named last changes fastest.
Arguments:
- tracer: float32 [8, 256, 4096], P(None, 'lat', 'lon'), may hold values from -6 to 6
- u_vel: float32 [8, 256, 4096], P(None, 'lat', 'lon'), may hold values from -6 to 6
- v_vel: float32 [8, 256, 4096], P(None, 'lat', 'lon'), may hold values from -6 to 6
- surface: float32 [256, 4096], P('lat', 'lon'), may hold values from -6 to 6
- land_mask: int32 [8, 256, 4096], P(None, 'lat', 'lon'), may hold values 0 or 1
- bottom: int32 [256, 4096], P('lat', 'lon'), may hold values from 1 to 8
- w_in: bfloat16 [24, 128], replicated, may hold values from -1.25 to 1.25
- b_in: float32 [128], replicated, may hold values from -4 to 4
- w_mid: bfloat16 [128, 128], replicated, may hold values from -0.5 to 0.5
- b_mid: float32 [128], replicated, may hold values from -4 to 4
- w_out: bfloat16 [128, 8], replicated, may hold values from -0.5 to 0.5
Outputs:
- tracer_new: float32 [8, 256, 4096], P(None, 'lat', 'lon')
- u_new: float32 [8, 256, 4096], P(None, 'lat', 'lon')
- v_new: float32 [8, 256, 4096], P(None, 'lat', 'lon')
- surface_new: float32 [256, 4096], P('lat', 'lon')
All inputs are finite; a program needn't handle non-finite values. No bound on the sum of `land_mask` on one device may be relied on, other than what follows from the above.
Results may differ from a plain program's by a relative error of at most 0.00034.
Values sent between devices are 32-bit elements; how exact they have to be, the bound alone decides.
A program may use at most 128 MiB of HBM per device.

v0:
```python
import jax
import jax.numpy as jnp
from jax import lax
from jax.sharding import PartitionSpec as P

ITERS = 3


def extended(block, sides, width):
    for axis, dim in sides:
        count = lax.axis_size(axis)
        forward = [(i, i + 1) for i in range(count - 1)]
        forward.append((count - 1, 0))
        backward = [(target, source) for source, target in forward]
        low = lax.ppermute(
            lax.slice_in_dim(block, block.shape[dim] - width, None, axis=dim), axis, forward
        )
        high = lax.ppermute(lax.slice_in_dim(block, 0, width, axis=dim), axis, backward)
        block = jnp.concatenate([low, block, high], axis=dim)
    return block


def edge_rows(ext, lat_index, lat_count):
    count = ext.shape[-2]
    row_ids = lax.broadcasted_iota(jnp.int32, (count, 1), 0)
    drop = jnp.logical_or(
        jnp.logical_and(row_ids == 0, lat_index == 0),
        jnp.logical_and(row_ids == count - 1, lat_index == lat_count - 1),
    )
    return ext * jnp.logical_not(drop).astype(jnp.float32)


def centre(e):
    return e[..., 1:-1, 1:-1]


def east_of(e):
    return e[..., 1:-1, 2:]


def west_of(e):
    return e[..., 1:-1, :-2]


def north_of(e):
    return e[..., 2:, 1:-1]


def south_of(e):
    return e[..., :-2, 1:-1]


def momentum(u_vel, v_vel, wet, floor, coriolis):
    u_star = u_vel + 0.2 * wet * (coriolis * v_vel - 0.5 * floor * u_vel)
    v_star = v_vel + 0.2 * wet * (-coriolis * u_vel - 0.5 * floor * v_vel)
    return (u_star, v_star)


def solve(rims, apply_op, total, rhs, start, precond):
    x = start
    x_ext = rims(x)
    resid = rhs - apply_op(x, x_ext)
    z = resid / precond
    p = z
    rz = total(jnp.sum(resid * z))
    for step in range(ITERS):
        p_ext = rims(p)
        q = apply_op(p, p_ext)
        alpha = rz / total(jnp.sum(p * q))
        x = x + alpha * p
        resid = resid - alpha * q
        z = resid / precond
        rz_new = total(jnp.sum(resid * z))
        p = z + rz_new / rz * p
        rz = rz_new
    x_ext = rims(x)
    return (x, x_ext)


def on_device(tracer, u_vel, v_vel, surface, land_mask, bottom, w_in, b_in, w_mid, b_mid, w_out):
    levels, rows, cols = tracer.shape
    lat_index = lax.axis_index("lat")
    lat_count = lax.axis_size("lat")
    total_rows = rows * lat_count
    level_ids = lax.broadcasted_iota(jnp.int32, (levels, 1, 1), 0)
    level_float = level_ids.astype(jnp.float32)
    wet = (land_mask * (level_ids < bottom[None]).astype(jnp.int32)).astype(jnp.float32)
    bottom_float = bottom.astype(jnp.float32)
    extra = []
    stacked = jnp.concatenate([tracer, u_vel, v_vel, wet, bottom_float[None]] + extra, axis=0)
    ext = extended(stacked, (("lon", 2), ("lat", 1)), 1)
    ext = edge_rows(ext, lat_index, lat_count)
    tracer_ext = ext[:levels]
    u_ext = ext[levels : 2 * levels]
    v_ext = ext[2 * levels : 3 * levels]
    wet_ext = ext[3 * levels : 4 * levels]
    floor_ext = (level_float == ext[4 * levels : 4 * levels + 1] - 1.0).astype(jnp.float32)
    ids = (lat_index * rows - 1 + lax.broadcasted_iota(jnp.int32, (rows + 2, 1), 0)).astype(
        jnp.float32
    )
    coriolis_ext = 2.0 * (ids + 0.5) / total_rows - 1.0
    ustar_ext, vstar_ext = momentum(u_ext, v_ext, wet_ext, floor_ext, coriolis_ext)
    trans_u_ext = jnp.sum(wet_ext * ustar_ext, axis=0)
    trans_v_ext = jnp.sum(wet_ext * vstar_ext, axis=0)
    depth_ext = jnp.sum(wet_ext, axis=0)
    u_star = centre(ustar_ext)
    v_star = centre(vstar_ext)
    lap = east_of(wet_ext) * (east_of(tracer_ext) - tracer) + west_of(wet_ext) * (
        west_of(tracer_ext) - tracer
    )
    lap = (
        lap
        + north_of(wet_ext) * (north_of(tracer_ext) - tracer)
        + south_of(wet_ext) * (south_of(tracer_ext) - tracer)
    )
    masked_ext = wet_ext * tracer_ext
    adv = -0.5 * (
        u_vel * (east_of(masked_ext) - west_of(masked_ext))
        + v_vel * (north_of(masked_ext) - south_of(masked_ext))
    )
    features = (
        jnp.concatenate([tracer, u_vel, v_vel], axis=0)
        .astype(jnp.bfloat16)
        .reshape(3 * levels, rows * cols)
    )
    first = jnp.dot(w_in.T, features, preferred_element_type=jnp.float32)
    hidden_one = jnp.tanh(first + b_in[:, None]).astype(jnp.bfloat16)
    second = jnp.dot(w_mid.T, hidden_one, preferred_element_type=jnp.float32)
    hidden_two = jnp.tanh(second + b_mid[:, None]).astype(jnp.bfloat16)
    closure = jnp.dot(w_out.T, hidden_two, preferred_element_type=jnp.float32).reshape(
        levels, rows, cols
    )
    tracer_new = tracer + 0.2 * wet * (lap + adv + closure)
    div = 0.5 * (
        east_of(trans_u_ext) - west_of(trans_u_ext) + north_of(trans_v_ext) - south_of(trans_v_ext)
    )
    depth_mid = centre(depth_ext)
    face_e = jnp.minimum(depth_mid, east_of(depth_ext))
    face_w = jnp.minimum(depth_mid, west_of(depth_ext))
    face_n = jnp.minimum(depth_mid, north_of(depth_ext))
    face_s = jnp.minimum(depth_mid, south_of(depth_ext))
    precond = 1.0 + face_e + face_w + face_n + face_s
    rhs = surface - div

    def surface_rims(x):
        return edge_rows(extended(x, (("lon", 1), ("lat", 0)), 1), lat_index, lat_count)

    def apply_tile(x, e):
        out = x + face_e * (x - east_of(e)) + face_w * (x - west_of(e))
        return out + face_n * (x - north_of(e)) + face_s * (x - south_of(e))

    def total(value):
        return lax.psum(value, ("lon", "lat"))

    solved, final_ext = solve(surface_rims, apply_tile, total, rhs, surface, precond)
    grad_x = east_of(final_ext) - west_of(final_ext)
    grad_y = north_of(final_ext) - south_of(final_ext)
    u_new = wet * (u_star - 0.5 * grad_x)
    v_new = wet * (v_star - 0.5 * grad_y)
    return (tracer_new, u_new, v_new, solved)


def solution(mesh):
    return jax.shard_map(
        on_device,
        mesh=mesh,
        in_specs=(
            P(None, "lat", "lon"),
            P(None, "lat", "lon"),
            P(None, "lat", "lon"),
            P("lat", "lon"),
            P(None, "lat", "lon"),
            P("lat", "lon"),
            P(),
            P(),
            P(),
            P(),
            P(),
        ),
        out_specs=(
            P(None, "lat", "lon"),
            P(None, "lat", "lon"),
            P(None, "lat", "lon"),
            P("lat", "lon"),
        ),
        check_vma=False,
    )
```

profile of v0, /device:TPU:0, one launch (start us, length us, event | category | flops | bytes accessed | tf_op | source)
XLA Modules:
  0.0 327.4 jit_solution(8152724755376744089)
XLA Ops:
  0.7 1.7 fusion.88
  2.9 5.0 %collective-permute-start.5 = (f32[128,1]{1,0:T(8,128)}, f32[128,1]{1,0:T(8,128)S(1)}, u32[]{:S(2)}, u32[]{:S(2)}) collective-permute-start(f32[128,1]{1,0:T(8,128)} %get-tuple-element.64), channel_id=1, source_target_pairs={{2,0},{4,2},{6,4},{8,6},{10,8},{12,10},{14,12},{16,14},{18,16},{20... | collective-permute-start | bytes 1544 | tf_op jit(solution)/shard_map/ppermute | solution.py:18
  7.8 2.7 convert_bitcast_fusion.2
  10.5 0.9 convert_bitcast_fusion.1
  12.6 2.6 fusion.83
  15.3 2.4 copy.36
  18.4 1.4 copy.35
  21.6 1.8 collective-permute-start.6
  23.6 2.3 collective-permute-done
  26.6 2.1 copy.38
  28.6 1.7 pad_maximum_fusion.2
  30.3 1.6 collective-permute-start.2
  33.3 1.2 collective-permute-done.2
  34.5 1.5 collective-permute-done.3
  36.0 3.5 %maximum_multiply_fusion = f32[33,130,258]{2,1,0:T(8,128)S(1)} fusion(f32[33,1,258]{2,1,0:T(1,128)S(1)} %collective-permute-done.3, f32[33,128,1]{2,1,0:T(8,128)S(1)} %copy-done.3, f32[33,128,256]{2,1,0:T(8,128)S(1)} %bitcast.21, f32[33,128,1]{2,1,0:T(8,128)S(1)} %copy.37, f32[33,1,258]{2,1,0:T(1,128)S(1)} %collective-permute-done.2, f32[130]{0:T(256)S(1)} %not_convert_fusion), kind=kLoop, calls=%fused_computation.6 | loop fusion | flops 5534100 | bytes 8855080 | tf_op jit(solution)/shard_map/mul | solution.py:30
  39.5 3.5 %multiply_reduce_fusion.1 = (f32[130,258]{1,0:T(8,128)S(1)}, f32[130,258]{1,0:T(8,128)S(1)}, f32[130,258]{1,0:T(8,128)S(1)}, f32[8,130,258]{2,1,0:T(8,128)}, f32...) fusion(f32[33,130,258]{2,1,0:T(8,128)S(1)} %maximum_multiply_fusion, f32[130,258]{1,0:T(8,128)S(1)} %fusion.34, ...), kind=kLoop, calls=%fused_computation.18 | loop fusion | flops 4997460 | bytes 8050672 | tf_op jit(solution)/shard_map/reduce_sum | solution.py:103
  43.3 1.1 fusion.79
  44.5 4.4 %collective-permute-start.9 = (f32[128,1]{1,0:T(8,128)S(1)}, f32[128,1]{1,0:T(8,128)S(1)}, u32[]{:S(2)}, u32[]{:S(2)}) collective-permute-start(f32[128,1]{1,0:T(8,128)S(1)} %get-tuple-element.62), channel_id=1, source_target_pairs={{2,0},{4,2},{6,4},{8,6},{10,8},{12,10},{14,12},{16,14},{18,16},{20... | collective-permute-start | bytes 1544 | tf_op jit(solution)/shard_map/ppermute | solution.py:18
  49.0 1.9 collective-permute-done.8
  51.5 1.5 collective-permute-start.11
  53.0 1.6 collective-permute-done.10
  55.3 1.5 multiply_reduce_fusion.5
  56.8 37.6 %all-reduce = (f32[]{:T(128)}, f32[]{:T(128)}) all-reduce(f32[]{:T(128)} %get-tuple-element.12, f32[]{:T(128)} %get-tuple-element.11), channel_id=1, replica_groups=mesh['lon'=16,'lat'=2] {'lon','lat'}, use_global_device_ids=true, to_apply=%region_4.0 | all-reduce | flops 2 | bytes 16 | tf_op jit(solution)/shard_map/psum | solution.py:153
  95.7 2.3 multiply_reduce_fusion.4
  98.0 42.2 %psum.44 = f32[]{:T(128)} all-reduce(f32[]{:T(128)} %get-tuple-element.17), channel_id=1, replica_groups=mesh['lon'=16,'lat'=2] {'lon','lat'}, use_global_device_ids=true, to_apply=%region_8.0 | all-reduce | flops 1 | bytes 8 | tf_op jit(solution)/shard_map/psum | solution.py:153
  141.7 4.4 %collective-permute-start.13 = (f32[128,1]{1,0:T(8,128)S(1)}, f32[128,1]{1,0:T(8,128)S(1)}, u32[]{:S(2)}, u32[]{:S(2)}) collective-permute-start(f32[128,1]{1,0:T(8,128)S(1)} %get-tuple-element.60), channel_id=1, source_target_pairs={{2,0},{4,2},{6,4},{8,6},{10,8},{12,10},{14,12},{16,14},{18,16},{20... | collective-permute-start | bytes 1544 | tf_op jit(solution)/shard_map/ppermute | solution.py:18
  146.1 2.0 collective-permute-done.12
  148.2 2.4 collective-permute-start.14
  150.8 1.5 collective-permute-done.14
  152.2 2.0 collective-permute-done.15
  154.4 2.5 multiply_reduce_fusion.3
  156.9 37.4 %psum.45 = f32[]{:T(128)} all-reduce(f32[]{:T(128)} %get-tuple-element.15), channel_id=1, replica_groups=mesh['lon'=16,'lat'=2] {'lon','lat'}, use_global_device_ids=true, to_apply=%region_10.0 | all-reduce | flops 1 | bytes 8 | tf_op jit(solution)/shard_map/psum | solution.py:153
  195.6 1.7 multiply_reduce_fusion.2
  197.3 41.1 %psum.46 = f32[]{:T(128)} all-reduce(f32[]{:T(128)} %multiply_reduce_fusion.2), channel_id=1, replica_groups=mesh['lon'=16,'lat'=2] {'lon','lat'}, use_global_device_ids=true, to_apply=%region_12.0 | all-reduce | flops 1 | bytes 8 | tf_op jit(solution)/shard_map/psum | solution.py:153
  239.7 1.1 multiply_add_fusion.1
  241.0 4.4 %collective-permute-start.17 = (f32[128,1]{1,0:T(8,128)S(1)}, f32[128,1]{1,0:T(8,128)S(1)}, u32[]{:S(2)}, u32[]{:S(2)}) collective-permute-start(f32[128,1]{1,0:T(8,128)S(1)} %get-tuple-element.58), channel_id=1, source_target_pairs={{2,0},{4,2},{6,4},{8,6},{10,8},{12,10},{14,12},{16,14},{18,16},{20... | collective-permute-start | bytes 1544 | tf_op jit(solution)/shard_map/ppermute | solution.py:18
  245.5 2.0 collective-permute-done.16
  247.6 2.5 collective-permute-start.18
  250.1 1.3 copy.40
  251.5 1.3 copy.41
  253.8 1.8 fusion.40
  255.6 5.1 %fusion.1 = bf16[32768,128]{1,0:T(8,128)(2,1)} fusion(bf16[24,128]{1,0:T(8,128)(2,1)S(1)} %copy-done.26, f32[128]{0:T(128)S(1)} %copy-done.28, bf16[8,32768]{1,0:T(8,128)(2,1)S(1)} %bitcast.25, bf16[8,32768]{1,0:T(8,128)(2,1)S(1)} %bitcast.24, bf16[8,32768]{1,0:T(8,128)(2,1)S(1)} %bitcast.23), kind=kOutput, calls=%fused_computation.2 | convolution fusion | flops 214433792 | bytes 9968128 | tf_op jit(solution)/shard_map/dot_general | solution.py:126
  260.8 38.0 %psum.47 = f32[]{:T(128)} all-reduce(f32[]{:T(128)} %fusion.40), channel_id=1, replica_groups=mesh['lon'=16,'lat'=2] {'lon','lat'}, use_global_device_ids=true, to_apply=%region_14.0 | all-reduce | flops 1 | bytes 8 | tf_op jit(solution)/shard_map/psum | solution.py:153
  300.3 4.4 %collective-permute-start.21 = (f32[128,1]{1,0:T(8,128)S(1)}, f32[128,1]{1,0:T(8,128)S(1)}, u32[]{:S(2)}, u32[]{:S(2)}) collective-permute-start(f32[128,1]{1,0:T(8,128)S(1)} %get-tuple-element.56), channel_id=1, source_target_pairs={{2,0},{4,2},{6,4},{8,6},{10,8},{12,10},{14,12},{16,14},{18,16},{20... | collective-permute-start | bytes 1544 | tf_op jit(solution)/shard_map/ppermute | solution.py:18
  304.7 7.9 %fusion.4 = f32[32768,8]{0,1:T(8,128)} fusion(bf16[128,8]{0,1:T(8,128)(2,1)S(1)} %copy-done.27, bf16[32768,128]{1,0:T(8,128)(2,1)} %fusion.1, bf16[128,128]{1,0:T(8,128)(2,1)S(1)} %copy-done, f32[128]{0:T(128)S(1)} %copy-done.29), kind=kOutput, calls=%fused_computation.7 | convolution fusion | flops 1149239296 | bytes 9472512 | tf_op jit(solution)/shard_map/dot_general | solution.py:130
  312.7 2.5 collective-permute-start.22
  315.3 9.7 %fusion.24 = f32[8,128,256]{2,1,0:T(8,128)} fusion(f32[8,128,256]{2,1,0:T(8,128)} %param.11, f32[8,128,256]{2,1,0:T(8,128)} %param.13, f32[8,130,258]{2,1,0:T(8,128)S(1)} %get-tuple-element.32, f32[8,128,256]{2,1,0:T(8,128)} %param.12, f32[33,130,258]{2,1,0:T(8,128)} %copy-done.1, f32[8,128,256]{2,0,1:T(8,128)} %bitcast.22, s32[8,128,256]{2,1,0:T(8,128)S(1)} %copy-done.4, ...), kind=kLoop, calls=%fused_computation.36 | loop fusion | flops 6553600 | bytes 19005440 | tf_op jit(solution)/shard_map/add | solution.py:133
  325.3 2.1 fusion.16
  (119 shorter events, 10.6 us)
Async XLA Ops:
  0.6 304.1 %copy-start = (bf16[128,128]{1,0:T(8,128)(2,1)S(1)}, bf16[128,128]{1,0:T(8,128)(2,1)}, u32[]{:S(2)}) copy-start(bf16[128,128]{1,0:T(8,128)(2,1)} %param.19) | copy-start | bytes 98308
  0.6 9.8 %copy-start.8 = (f32[8,128,256]{2,1,0:T(8,128)S(1)}, f32[8,128,256]{2,1,0:T(8,128)}, u32[]{:S(2)}) copy-start(f32[8,128,256]{2,1,0:T(8,128)} %param.12) | copy-start | bytes 3145732
  0.7 10.8 %copy-start.7 = (f32[8,128,256]{2,1,0:T(8,128)S(1)}, f32[8,128,256]{2,1,0:T(8,128)}, u32[]{:S(2)}) copy-start(f32[8,128,256]{2,1,0:T(8,128)} %param.13) | copy-start | bytes 3145732
  2.4 18.5 %collective-permute-start.4 = (f32[128,1]{1,0:T(8,128)}, f32[128,1]{1,0:T(8,128)S(1)}, u32[]{:S(2)}, u32[]{:S(2)}) collective-permute-start(f32[128,1]{1,0:T(8,128)} %get-tuple-element.63), channel_id=1, source_target_pairs={{0,2},{2,4},{4,6},{6,8},{8,10},{10,12},{12,14},{14,16},{16,18},{18... | collective-permute-start | bytes 1544 | tf_op jit(solution)/shard_map/ppermute | solution.py:15
  2.9 18.0 %collective-permute-start.5 = (f32[128,1]{1,0:T(8,128)}, f32[128,1]{1,0:T(8,128)S(1)}, u32[]{:S(2)}, u32[]{:S(2)}) collective-permute-start(f32[128,1]{1,0:T(8,128)} %get-tuple-element.64), channel_id=1, source_target_pairs={{2,0},{4,2},{6,4},{8,6},{10,8},{12,10},{14,12},{16,14},{18,16},{20... | collective-permute-start | bytes 1544 | tf_op jit(solution)/shard_map/ppermute | solution.py:18
  15.3 5.6 %copy-start.9 = (f32[128,256]{1,0:T(8,128)S(1)}, f32[128,256]{1,0:T(8,128)}, u32[]{:S(2)}) copy-start(f32[128,256]{1,0:T(8,128)} %param.14) | copy-start | bytes 393220
  17.7 8.9 %collective-permute-start.1 = (f32[33,128,1]{1,0,2:T(8,128)S(1)}, f32[33,128,1]{1,0,2:T(8,128)S(1)}, u32[]{:S(2)}, u32[]{:S(2)}) collective-permute-start(f32[33,128,1]{1,0,2:T(8,128)S(1)} %copy.36), channel_id=1, source_target_pairs={{2,0},{4,2},{6,4},{8,6},{10,8},{12,10},{14,12},{16,14},{18,16},{20... | collective-permute-start | bytes 50696 | tf_op jit(solution)/shard_map/ppermute | solution.py:18
  19.7 6.1 %collective-permute-start = (f32[33,128,1]{1,0,2:T(8,128)}, f32[33,128,1]{1,0,2:T(8,128)S(1)}, u32[]{:S(2)}, u32[]{:S(2)}) collective-permute-start(f32[33,128,1]{1,0,2:T(8,128)} %copy.35), channel_id=1, source_target_pairs={{0,2},{2,4},{4,6},{6,8},{8,10},{10,12},{12,14},{14,16},{16,18},{18... | collective-permute-start | bytes 50696 | tf_op jit(solution)/shard_map/ppermute | solution.py:15
  21.6 10.8 %collective-permute-start.6 = (f32[1,258]{1,0:T(1,128)}, f32[1,258]{1,0:T(1,128)}, u32[]{:S(2)}, u32[]{:S(2)}) collective-permute-start(f32[1,258]{1,0:T(1,128)} %get-tuple-element.51), channel_id=1, source_target_pairs={{0,1},{1,0},{2,3},{3,2},{4,5},{5,4},{6,7},{7,6},{8,9},{9,8},{10,11... | collective-permute-start | bytes 3104 | tf_op jit(solution)/shard_map/ppermute | solution.py:15
  23.4 9.0 %collective-permute-start.7 = (f32[1,258]{1,0:T(1,128)}, f32[1,258]{1,0:T(1,128)}, u32[]{:S(2)}, u32[]{:S(2)}) collective-permute-start(f32[1,258]{1,0:T(1,128)} %get-tuple-element.52), channel_id=1, source_target_pairs={{1,0},{0,1},{3,2},{2,3},{5,4},{4,5},{7,6},{6,7},{9,8},{8,9},{11,10... | collective-permute-start | bytes 3104 | tf_op jit(solution)/shard_map/ppermute | solution.py:18
  26.5 9.4 %slice-start = ((s8[4325376]{0:T(1024)(128)(4,1)}), s8[131072]{0:T(1024)(128)(4,1)S(1)}, s32[]{:S(2)}) async-start(s8[4325376]{0:T(1024)(128)(4,1)} %bitcast.20), calls=%async_computation | async-start | bytes 262144
  28.6 7.4 %slice-start.1 = ((s8[4325376]{0:T(1024)(128)(4,1)}), s8[4194304]{0:T(1024)(128)(4,1)S(1)}, s32[]{:S(2)}) async-start(s8[4325376]{0:T(1024)(128)(4,1)} %bitcast.20), calls=%async_computation.1 | async-start | bytes 8388608
  28.6 7.4 %copy-start.3 = (f32[33,128,1]{2,1,0:T(8,128)S(1)}, f32[33,128,1]{2,1,0:T(8,128)}, u32[]{:S(2)}) copy-start(f32[33,128,1]{2,1,0:T(8,128)} %copy.38) | copy-start | bytes 50692
  30.3 4.2 %collective-permute-start.2 = (f32[33,1,258]{2,1,0:T(1,128)S(1)}, f32[33,1,258]{2,1,0:T(1,128)S(1)}, u32[]{:S(2)}, u32[]{:S(2)}) collective-permute-start(f32[33,1,258]{2,1,0:T(1,128)S(1)} %get-tuple-element.30), channel_id=1, source_target_pairs={{0,1},{1,0},{2,3},{3,2},{4,5},{5,4},{6,7},{7,6},{8,9},{9,8},{10,11... | collective-permute-start | bytes 102176 | tf_op jit(solution)/shard_map/ppermute | solution.py:15
  31.9 4.1 %collective-permute-start.3 = (f32[33,1,258]{2,1,0:T(1,128)S(1)}, f32[33,1,258]{2,1,0:T(1,128)S(1)}, u32[]{:S(2)}, u32[]{:S(2)}) collective-permute-start(f32[33,1,258]{2,1,0:T(1,128)S(1)} %get-tuple-element.31), channel_id=1, source_target_pairs={{1,0},{0,1},{3,2},{2,3},{5,4},{4,5},{7,6},{6,7},{9,8},{8,9},{11,10... | collective-permute-start | bytes 102176 | tf_op jit(solution)/shard_map/ppermute | solution.py:18
  33.2 6.3 %copy-start.24 = (f32[130]{0:T(256)S(1)}, f32[130]{0:T(256)}, u32[]{:S(2)}) copy-start(f32[130]{0:T(256)} %get-tuple-element.66) | copy-start | bytes 1564
  33.3 6.3 %copy-start.25 = (f32[8]{0:T(128)S(1)}, f32[8]{0:T(128)}, u32[]{:S(2)}) copy-start(f32[8]{0:T(128)} %iota_convert_fusion) | copy-start | bytes 100
  44.4 12.4 %copy-start.17 = (f32[128,256]{1,0:T(8,128)}, f32[128,256]{1,0:T(8,128)S(1)}, u32[]{:S(2)}) copy-start(f32[128,256]{1,0:T(8,128)S(1)} %get-tuple-element.26) | copy-start | bytes 393220
  44.4 12.4 %copy-start.18 = (f32[128,256]{1,0:T(8,128)}, f32[128,256]{1,0:T(8,128)S(1)}, u32[]{:S(2)}) copy-start(f32[128,256]{1,0:T(8,128)S(1)} %get-tuple-element.27) | copy-start | bytes 393220
  44.4 12.4 %copy-start.19 = (f32[128,256]{1,0:T(8,128)}, f32[128,256]{1,0:T(8,128)S(1)}, u32[]{:S(2)}) copy-start(f32[128,256]{1,0:T(8,128)S(1)} %get-tuple-element.23) | copy-start | bytes 393220
  44.4 97.1 %copy-start.16 = (f32[128,256]{1,0:T(8,128)}, f32[128,256]{1,0:T(8,128)S(1)}, u32[]{:S(2)}) copy-start(f32[128,256]{1,0:T(8,128)S(1)} %get-tuple-element.25) | copy-start | bytes 393220
  44.4 196.5 %copy-start.14 = (f32[128,256]{1,0:T(8,128)}, f32[128,256]{1,0:T(8,128)S(1)}, u32[]{:S(2)}) copy-start(f32[128,256]{1,0:T(8,128)S(1)} %get-tuple-element.24) | copy-start | bytes 393220
  44.5 6.4 %collective-permute-start.8 = (f32[128,1]{1,0:T(8,128)S(1)}, f32[128,1]{1,0:T(8,128)S(1)}, u32[]{:S(2)}, u32[]{:S(2)}) collective-permute-start(f32[128,1]{1,0:T(8,128)S(1)} %get-tuple-element.61), channel_id=1, source_target_pairs={{0,2},{2,4},{4,6},{6,8},{8,10},{10,12},{12,14},{14,16},{16,18},{18... | collective-permute-start | bytes 1544 | tf_op jit(solution)/shard_map/ppermute | solution.py:15
  44.5 6.4 %collective-permute-start.9 = (f32[128,1]{1,0:T(8,128)S(1)}, f32[128,1]{1,0:T(8,128)S(1)}, u32[]{:S(2)}, u32[]{:S(2)}) collective-permute-start(f32[128,1]{1,0:T(8,128)S(1)} %get-tuple-element.62), channel_id=1, source_target_pairs={{2,0},{4,2},{6,4},{8,6},{10,8},{12,10},{14,12},{16,14},{18,16},{20... | collective-permute-start | bytes 1544 | tf_op jit(solution)/shard_map/ppermute | solution.py:18
  51.0 3.6 %collective-permute-start.10 = (f32[1,258]{1,0:T(1,128)S(1)}, f32[1,258]{1,0:T(1,128)S(1)}, u32[]{:S(2)}, u32[]{:S(2)}) collective-permute-start(f32[1,258]{1,0:T(1,128)S(1)} %get-tuple-element.49), channel_id=1, source_target_pairs={{0,1},{1,0},{2,3},{3,2},{4,5},{5,4},{6,7},{7,6},{8,9},{9,8},{10,11... | collective-permute-start | bytes 3104 | tf_op jit(solution)/shard_map/ppermute | solution.py:15
  51.5 3.6 %collective-permute-start.11 = (f32[1,258]{1,0:T(1,128)S(1)}, f32[1,258]{1,0:T(1,128)S(1)}, u32[]{:S(2)}, u32[]{:S(2)}) collective-permute-start(f32[1,258]{1,0:T(1,128)S(1)} %get-tuple-element.50), channel_id=1, source_target_pairs={{1,0},{0,1},{3,2},{2,3},{5,4},{4,5},{7,6},{6,7},{9,8},{8,9},{11,10... | collective-permute-start | bytes 3104 | tf_op jit(solution)/shard_map/ppermute | solution.py:18
  141.6 6.5 %collective-permute-start.12 = (f32[128,1]{1,0:T(8,128)S(1)}, f32[128,1]{1,0:T(8,128)S(1)}, u32[]{:S(2)}, u32[]{:S(2)}) collective-permute-start(f32[128,1]{1,0:T(8,128)S(1)} %get-tuple-element.59), channel_id=1, source_target_pairs={{0,2},{2,4},{4,6},{6,8},{8,10},{10,12},{12,14},{14,16},{16,18},{18... | collective-permute-start | bytes 1544 | tf_op jit(solution)/shard_map/ppermute | solution.py:15
  141.7 6.5 %collective-permute-start.13 = (f32[128,1]{1,0:T(8,128)S(1)}, f32[128,1]{1,0:T(8,128)S(1)}, u32[]{:S(2)}, u32[]{:S(2)}) collective-permute-start(f32[128,1]{1,0:T(8,128)S(1)} %get-tuple-element.60), channel_id=1, source_target_pairs={{2,0},{4,2},{6,4},{8,6},{10,8},{12,10},{14,12},{16,14},{18,16},{20... | collective-permute-start | bytes 1544 | tf_op jit(solution)/shard_map/ppermute | solution.py:18
  148.2 4.0 %collective-permute-start.14 = (f32[1,258]{1,0:T(1,128)S(1)}, f32[1,258]{1,0:T(1,128)S(1)}, u32[]{:S(2)}, u32[]{:S(2)}) collective-permute-start(f32[1,258]{1,0:T(1,128)S(1)} %get-tuple-element.47), channel_id=1, source_target_pairs={{0,1},{1,0},{2,3},{3,2},{4,5},{5,4},{6,7},{7,6},{8,9},{9,8},{10,11... | collective-permute-start | bytes 3104 | tf_op jit(solution)/shard_map/ppermute | solution.py:15
  150.7 3.6 %collective-permute-start.15 = (f32[1,258]{1,0:T(1,128)S(1)}, f32[1,258]{1,0:T(1,128)S(1)}, u32[]{:S(2)}, u32[]{:S(2)}) collective-permute-start(f32[1,258]{1,0:T(1,128)S(1)} %get-tuple-element.48), channel_id=1, source_target_pairs={{1,0},{0,1},{3,2},{2,3},{5,4},{4,5},{7,6},{6,7},{9,8},{8,9},{11,10... | collective-permute-start | bytes 3104 | tf_op jit(solution)/shard_map/ppermute | solution.py:18
  195.6 60.0 %copy-start.26 = (bf16[24,128]{1,0:T(8,128)(2,1)S(1)}, bf16[24,128]{1,0:T(8,128)(2,1)}, u32[]{:S(2)}) copy-start(bf16[24,128]{1,0:T(8,128)(2,1)} %param.17) | copy-start | bytes 18436
  195.6 60.0 %copy-start.28 = (f32[128]{0:T(128)S(1)}, f32[128]{0:T(128)}, u32[]{:S(2)}) copy-start(f32[128]{0:T(128)} %param.18) | copy-start | bytes 1540
  239.7 13.1 %copy-start.12 = (bf16[1,8,128,256]{3,2,1,0:T(8,128)(2,1)S(1)}, bf16[1,8,128,256]{3,2,1,0:T(8,128)(2,1)}, u32[]{:S(2)}) copy-start(bf16[1,8,128,256]{3,2,1,0:T(8,128)(2,1)} %get-tuple-element.41) | copy-start | bytes 1572868
  241.0 12.8 %copy-start.15 = (f32[128,256]{1,0:T(8,128)S(1)}, f32[128,256]{1,0:T(8,128)}, u32[]{:S(2)}) copy-start(f32[128,256]{1,0:T(8,128)} %copy-done.14) | copy-start | bytes 393220
  241.0 6.5 %collective-permute-start.16 = (f32[128,1]{1,0:T(8,128)S(1)}, f32[128,1]{1,0:T(8,128)S(1)}, u32[]{:S(2)}, u32[]{:S(2)}) collective-permute-start(f32[128,1]{1,0:T(8,128)S(1)} %get-tuple-element.57), channel_id=1, source_target_pairs={{0,2},{2,4},{4,6},{6,8},{8,10},{10,12},{12,14},{14,16},{16,18},{18... | collective-permute-start | bytes 1544 | tf_op jit(solution)/shard_map/ppermute | solution.py:15
  241.0 6.5 %collective-permute-start.17 = (f32[128,1]{1,0:T(8,128)S(1)}, f32[128,1]{1,0:T(8,128)S(1)}, u32[]{:S(2)}, u32[]{:S(2)}) collective-permute-start(f32[128,1]{1,0:T(8,128)S(1)} %get-tuple-element.58), channel_id=1, source_target_pairs={{2,0},{4,2},{6,4},{8,6},{10,8},{12,10},{14,12},{16,14},{18,16},{20... | collective-permute-start | bytes 1544 | tf_op jit(solution)/shard_map/ppermute | solution.py:18
  247.6 5.5 %collective-permute-start.18 = (f32[1,258]{1,0:T(1,128)S(1)}, f32[1,258]{1,0:T(1,128)S(1)}, u32[]{:S(2)}, u32[]{:S(2)}) collective-permute-start(f32[1,258]{1,0:T(1,128)S(1)} %get-tuple-element.45), channel_id=1, source_target_pairs={{0,1},{1,0},{2,3},{3,2},{4,5},{5,4},{6,7},{7,6},{8,9},{9,8},{10,11... | collective-permute-start | bytes 3104 | tf_op jit(solution)/shard_map/ppermute | solution.py:15
  250.1 3.6 %collective-permute-start.19 = (f32[1,258]{1,0:T(1,128)S(1)}, f32[1,258]{1,0:T(1,128)S(1)}, u32[]{:S(2)}, u32[]{:S(2)}) collective-permute-start(f32[1,258]{1,0:T(1,128)S(1)} %get-tuple-element.46), channel_id=1, source_target_pairs={{1,0},{0,1},{3,2},{2,3},{5,4},{4,5},{7,6},{6,7},{9,8},{8,9},{11,10... | collective-permute-start | bytes 3104 | tf_op jit(solution)/shard_map/ppermute | solution.py:18
  255.6 49.1 %copy-start.27 = (bf16[128,8]{0,1:T(8,128)(2,1)S(1)}, bf16[128,8]{0,1:T(8,128)(2,1)}, u32[]{:S(2)}) copy-start(bf16[128,8]{0,1:T(8,128)(2,1)} %param.21) | copy-start | bytes 6148
  255.6 49.1 %copy-start.29 = (f32[128]{0:T(128)S(1)}, f32[128]{0:T(128)}, u32[]{:S(2)}) copy-start(f32[128]{0:T(128)} %param.20) | copy-start | bytes 1540
  300.2 24.8 %copy-start.13 = (f32[128,256]{1,0:T(8,128)}, f32[128,256]{1,0:T(8,128)S(1)}, u32[]{:S(2)}) copy-start(f32[128,256]{1,0:T(8,128)S(1)} %multiply_add_fusion) | copy-start | bytes 393220
  300.3 12.4 %collective-permute-start.20 = (f32[128,1]{1,0:T(8,128)S(1)}, f32[128,1]{1,0:T(8,128)S(1)}, u32[]{:S(2)}, u32[]{:S(2)}) collective-permute-start(f32[128,1]{1,0:T(8,128)S(1)} %get-tuple-element.55), channel_id=1, source_target_pairs={{0,2},{2,4},{4,6},{6,8},{8,10},{10,12},{12,14},{14,16},{16,18},{18... | collective-permute-start | bytes 1544 | tf_op jit(solution)/shard_map/ppermute | solution.py:15
  300.3 15.0 %copy-start.11 = (s32[128,256]{1,0:T(8,128)S(1)}, s32[128,256]{1,0:T(8,128)}, u32[]{:S(2)}) copy-start(s32[128,256]{1,0:T(8,128)} %param.16) | copy-start | bytes 393220
  300.3 12.3 %collective-permute-start.21 = (f32[128,1]{1,0:T(8,128)S(1)}, f32[128,1]{1,0:T(8,128)S(1)}, u32[]{:S(2)}, u32[]{:S(2)}) collective-permute-start(f32[128,1]{1,0:T(8,128)S(1)} %get-tuple-element.56), channel_id=1, source_target_pairs={{2,0},{4,2},{6,4},{8,6},{10,8},{12,10},{14,12},{16,14},{18,16},{20... | collective-permute-start | bytes 1544 | tf_op jit(solution)/shard_map/ppermute | solution.py:18
  312.7 12.2 %collective-permute-start.22 = (f32[1,258]{1,0:T(1,128)S(1)}, f32[1,258]{1,0:T(1,128)S(1)}, u32[]{:S(2)}, u32[]{:S(2)}) collective-permute-start(f32[1,258]{1,0:T(1,128)S(1)} %get-tuple-element.43), channel_id=1, source_target_pairs={{0,1},{1,0},{2,3},{3,2},{4,5},{5,4},{6,7},{7,6},{8,9},{9,8},{10,11... | collective-permute-start | bytes 3104 | tf_op jit(solution)/shard_map/ppermute | solution.py:15
  315.2 9.8 %collective-permute-start.23 = (f32[1,258]{1,0:T(1,128)S(1)}, f32[1,258]{1,0:T(1,128)S(1)}, u32[]{:S(2)}, u32[]{:S(2)}) collective-permute-start(f32[1,258]{1,0:T(1,128)S(1)} %get-tuple-element.44), channel_id=1, source_target_pairs={{1,0},{0,1},{3,2},{2,3},{5,4},{4,5},{7,6},{6,7},{9,8},{8,9},{11,10... | collective-permute-start | bytes 3104 | tf_op jit(solution)/shard_map/ppermute | solution.py:18
  315.3 10.0 %copy-start.5 = (f32[8,130,258]{2,1,0:T(8,128)S(1)}, f32[8,130,258]{2,1,0:T(8,128)}, u32[]{:S(2)}) copy-start(f32[8,130,258]{2,1,0:T(8,128)} %get-tuple-element.28) | copy-start | bytes 3219844
  315.3 10.0 %copy-start.6 = (f32[8,130,258]{2,1,0:T(8,128)S(1)}, f32[8,130,258]{2,1,0:T(8,128)}, u32[]{:S(2)}) copy-start(f32[8,130,258]{2,1,0:T(8,128)} %get-tuple-element.29) | copy-start | bytes 3219844
  (8 other events, 23.4 us)
where the time goes:
time: 329 us; the launch traced here: 327 us
  blocking collectives  196 us (60%)
  other arithmetic  40.8 us (12%)
  starting transfers between devices  37.7 us (11%)
  waiting for transfers between devices  17.1 us (5%)
  local copies, waits for them, and re-layouts  14.7 us (4%)
  matrix products  13 us (4%)
  between operations  7.62 us (2%)
    psum x5, blocking collectives, total(): return lax.psum(value, ('lon', 'lat'))  196 us
    ppermute x12, starting transfers between devices, extended(): lax.ppermute(lax.slice_in_dim(block, 0, width, axis=dim), axis, backward)  25.8 us
    ppermute x12, waiting for transfers between devices, extended(): lax.ppermute(lax.slice_in_dim(block, block.shape[dim] - width, None, axis...  12.5 us
    ppermute x12, starting transfers between devices, extended(): lax.ppermute(lax.slice_in_dim(block, block.shape[dim] - width, None, axis...  11.9 us
    add x1, other arithmetic, on_device(): tracer_new = tracer + 0.2 * wet * (lap + adv + closure)  9.66 us
    dot_general x1, matrix products, on_device(): jnp.dot(w_out.T, hidden_two, preferred_element_type=jnp.float32)  7.9 us
  transfers between devices with their start and end apart: 24, of which 11 were waited for; matrix products, arithmetic and copies ran while one was open for 12% of the time, Pallas kernels for 0%

commit v1 on v0

v1 whole, which is shorter than its diff:
```python
import functools

import jax
import jax.numpy as jnp
from jax import lax
from jax.experimental import pallas as pl
from jax.experimental.pallas import tpu as pltpu
from jax.sharding import PartitionSpec as P

MESH = pl.DeviceIdType.MESH
HALO = 4
F32 = jnp.float32
BF16 = jnp.bfloat16
NT = (((1,), (1,)), ((), ()))
TN = (((0,), (0,)), ((), ()))


def shift_to(x, offset, axis):
    return pltpu.roll(x, (-offset) % x.shape[axis], axis)


def inner(a, b, moments):
    out = None
    for i, ai in enumerate(a):
        for j, bj in enumerate(b):
            term = ai * bj * moments[i + j]
            out = term if out is None else out + term
    return out


def scaled_minus_shift(p):
    out = [p[0]]
    for lower, upper in zip(p[:-1], p[1:]):
        out.append(upper - lower)
    out.append(-p[-1])
    return out


def add_poly(a, scale, b):
    out = []
    for i in range(max(len(a), len(b))):
        if i >= len(a):
            out.append(scale * b[i])
        elif i >= len(b):
            out.append(a[i])
        else:
            out.append(a[i] + scale * b[i])
    return out


def cg_coefficients(moments, iters, top):
    one = jnp.ones_like(moments[0])
    z, p, x = [one], [one], [jnp.zeros_like(one)]
    rz = moments[0]
    for step in range(iters):
        q = scaled_minus_shift(p)
        pq = jnp.maximum(inner(p, q, moments), rz * (1.0 / top))
        alpha = rz / pq
        x = add_poly(x, alpha, p)
        if step == iters - 1:
            break
        z = add_poly(z, -alpha, q)
        rz_new = jnp.maximum(inner(z, z, moments), 1e-35)
        p = add_poly(z, rz_new / rz, p)
        rz = rz_new
    return x


def kernel(
    nlon, nlat,
    tr, uu, vv, surf, land, bot, w_in, b_in, w_mid, b_mid, w_out,
    tr_out, u_out, v_out, s_out,
    wet_s, msk_s, clo_s, X, U, V, D, zs, w1s, w2s,
    wbig, wmt, wob, bias1, bias2, h1, h2,
    pack_w, pack_e, row_n, row_s, recv_e, recv_w, recv_n, recv_s,
    red1, red2, halo_send, halo_recv, send1, recv1, send2, recv2,
):
    lev, rows, cols = tr.shape
    hid = w_mid.shape[0]
    lon, lat = lax.axis_index("lon"), lax.axis_index("lat")
    east, west = lax.rem(lon + 1, nlon), lax.rem(lon + nlon - 1, nlon)
    north, south = lax.rem(lat + 1, nlat), lax.rem(lat + nlat - 1, nlat)

    barrier = pltpu.get_barrier_semaphore()
    for d in range(1, nlon):
        pl.semaphore_signal(barrier, inc=1, device_id=(lax.rem(lon + d, nlon), lat), device_id_type=MESH)
    for d in range(1, nlat):
        pl.semaphore_signal(barrier, inc=1, device_id=(lon, lax.rem(lat + d, nlat)), device_id_type=MESH)
    for a in (east, west):
        for b in (north, south):
            pl.semaphore_signal(barrier, inc=1, device_id=(a, b), device_id_type=MESH)

    step = 8

    @pl.loop(0, rows // step)
    def _(g):
        r0 = pl.multiple_of(g * step, step)
        rs = pl.ds(r0, step)
        bottom = bot[rs, :]
        j = (lat * rows + r0 + lax.broadcasted_iota(jnp.int32, (step, 1), 0)).astype(F32)
        f = 2.0 * (j + 0.5) / (rows * nlat) - 1.0
        su = sv = sd = None
        for l in range(lev):
            wet = jnp.where(l < bottom, land[l, rs, :], 0).astype(F32)
            half_floor = jnp.where(bottom == l + 1, 0.5, 0.0)
            u, v = uu[l, rs, :], vv[l, rs, :]
            scaled = 0.2 * wet
            us = u + scaled * (f * v - half_floor * u)
            vs = v + scaled * (-f * u - half_floor * v)
            u_out[l, rs, :] = us
            v_out[l, rs, :] = vs
            wet_s[l, rs, :] = wet
            msk_s[l, rs, :] = wet * tr[l, rs, :]
            su = wet * us if su is None else su + wet * us
            sv = wet * vs if sv is None else sv + wet * vs
            sd = wet if sd is None else sd + wet
        U[rs, :cols] = su
        V[rs, :cols] = sv
        D[rs, :cols] = sd
        X[rs, :cols] = surf[rs, :]

    lane = lax.broadcasted_iota(jnp.int32, (rows, 128), 1)
    fields = (U, V, D, X)
    for pack, at, edge, width_at in ((pack_w, 0, 0, 0), (pack_e, cols - 128, 127, 128 - HALO)):
        acc = jnp.zeros((rows, 128), F32)
        for k, ref in enumerate(fields):
            moved = pltpu.roll(ref[:rows, at : at + 128], (HALO * k - width_at) % 128, 1)
            acc = jnp.where((lane >= HALO * k) & (lane < HALO * (k + 1)), moved, acc)
        for l in range(lev):
            for m, ref in enumerate((msk_s, wet_s)):
                to = HALO * 4 + m * lev + l
                moved = pltpu.roll(ref[l, :, at : at + 128], (to - edge) % 128, 1)
                acc = jnp.where(lane == to, moved, acc)
        pack[...] = acc
    for buf, at, edge in ((row_n, rows - 8, rows - 1), (row_s, 0, 0)):
        for k, ref in enumerate(fields):
            buf[8 * k : 8 * k + 8, :] = ref[at : at + 8, :cols]
        for l in range(lev):
            buf[32 + l : 33 + l, :] = msk_s[l, edge : edge + 1, :]
            buf[32 + lev + l : 33 + lev + l, :] = wet_s[l, edge : edge + 1, :]

    pl.semaphore_wait(barrier, nlon - 1 + nlat - 1 + 4)

    plan = (
        (pack_w, recv_e.at[pl.ds(0, rows)], (west, lat)),
        (pack_e, recv_w.at[pl.ds(0, rows)], (east, lat)),
        (row_n, recv_s, (lon, north)),
        (row_s, recv_n, (lon, south)),
        (pack_w.at[pl.ds(rows - 8, 8)], recv_e.at[pl.ds(rows + 8, 8)], (west, north)),
        (pack_e.at[pl.ds(rows - 8, 8)], recv_w.at[pl.ds(rows + 8, 8)], (east, north)),
        (pack_w.at[pl.ds(0, 8)], recv_e.at[pl.ds(rows, 8)], (west, south)),
        (pack_e.at[pl.ds(0, 8)], recv_w.at[pl.ds(rows, 8)], (east, south)),
    )
    halo_copies = []
    for i, (src, dst, dev) in enumerate(plan):
        halo_copies.append(pltpu.make_async_remote_copy(
            src_ref=src, dst_ref=dst, send_sem=halo_send.at[i], recv_sem=halo_recv.at[i],
            device_id=dev, device_id_type=MESH))
    for c in halo_copies:
        c.start()

    nf = w_in.shape[0]
    spread = (lax.broadcasted_iota(jnp.int32, (nf, nf * 8), 0)
              == lax.broadcasted_iota(jnp.int32, (nf, nf * 8), 1) // 8).astype(F32).astype(BF16)
    wide = lax.dot_general(w_in[...], spread, TN, preferred_element_type=F32)
    which = lax.broadcasted_iota(jnp.int32, wide.shape, 1) % 8
    for jj in range(8):
        wbig[jj * hid : (jj + 1) * hid, :] = jnp.where(which == jj, wide, 0.0).astype(BF16)
    eye = (lax.broadcasted_iota(jnp.int32, (hid, hid), 0)
           == lax.broadcasted_iota(jnp.int32, (hid, hid), 1))
    wmt[...] = lax.dot_general(w_mid[...], eye.astype(F32).astype(BF16), TN, preferred_element_type=F32).astype(BF16)
    pick = (lax.broadcasted_iota(jnp.int32, (lev * 8, lev), 0) // 8
            == lax.broadcasted_iota(jnp.int32, (lev * 8, lev), 1)).astype(F32).astype(BF16)
    tall = lax.dot_general(pick, w_out[...], NT, preferred_element_type=F32)
    which = lax.broadcasted_iota(jnp.int32, tall.shape, 0) % 8
    for jj in range(8):
        wob[:, jj * hid : (jj + 1) * hid] = jnp.where(which == jj, tall, 0.0).astype(BF16)
    for b, bias in ((b_in, bias1), (b_mid, bias2)):
        column = jnp.sum(jnp.where(eye, b[...], 0.0), axis=1, keepdims=True)
        bias[...] = jnp.broadcast_to(column, bias.shape)

    def network(g):
        rs = pl.ds(pl.multiple_of(g * 8, 8), 8)
        feats = jnp.concatenate(
            [ref[:, rs, :].reshape(lev * 8, cols) for ref in (tr, uu, vv)], axis=0).astype(BF16)
        for jj in range(8):
            at = slice(jj * hid, (jj + 1) * hid)
            first = jnp.dot(wbig[at, :], feats, preferred_element_type=F32)
            h1[at, :] = jnp.tanh(first + bias1[...]).astype(BF16)
        for jj in range(8):
            at = slice(jj * hid, (jj + 1) * hid)
            second = jnp.dot(wmt[...], h1[at, :], preferred_element_type=F32)
            h2[at, :] = jnp.tanh(second + bias2[...]).astype(BF16)
        out = jnp.dot(wob[...], h2[...], preferred_element_type=F32)
        clo_s[:, rs, :] = out.reshape(lev, 8, cols)

    groups = rows // 8
    cut1, cut2 = groups // 2, groups * 3 // 4
    pl.loop(0, cut1)(network)

    for c in halo_copies:
        c.wait_recv()

    open_n = jnp.where(lat == nlat - 1, 0.0, 1.0).astype(F32)
    open_s = jnp.where(lat == 0, 0.0, 1.0).astype(F32)
    ext_rows = rows + 16
    lane = lax.broadcasted_iota(jnp.int32, (ext_rows, 128), 1)
    row_id = lax.broadcasted_iota(jnp.int32, (ext_rows, 1), 0)
    inside = jnp.where(row_id < rows, 1.0, jnp.where(row_id < rows + 8, open_n, open_s))
    e_all, w_all = recv_e[...] * inside, recv_w[...] * inside
    for k, ref in enumerate(fields):
        side = jnp.where(lane < HALO, pltpu.roll(e_all, (-HALO * k) % 128, 1), 0.0)
        ref[:, cols:] = jnp.where(
            lane >= 128 - HALO, pltpu.roll(w_all, (128 - HALO - HALO * k) % 128, 1), side)
        ref[rows : rows + 8, :cols] = recv_n[8 * k : 8 * k + 8, :] * open_n
        ref[rows + 8 :, :cols] = recv_s[8 * k : 8 * k + 8, :] * open_s

    depth = D[...]
    face_e = jnp.minimum(depth, shift_to(depth, 1, 1))
    face_n = jnp.minimum(depth, shift_to(depth, 1, 0))
    face_w = shift_to(face_e, -1, 1)
    face_s = shift_to(face_n, -1, 0)
    precond = 1.0 + face_e + face_w + face_n + face_s
    inverse = 1.0 / precond

    def neighbours(x):
        return (face_e * shift_to(x, 1, 1) + face_w * shift_to(x, -1, 1)
                + face_n * shift_to(x, 1, 0) + face_s * shift_to(x, -1, 0))

    x0, ub, vb = X[...], U[...], V[...]
    div = 0.5 * (shift_to(ub, 1, 1) - shift_to(ub, -1, 1) + shift_to(vb, 1, 0) - shift_to(vb, -1, 0))
    resid = (x0 - div - precond * x0 + neighbours(x0)) * inside
    z0 = resid * inverse
    nz = neighbours(z0)
    w1 = nz * inverse
    nw1 = neighbours(w1)
    w2 = nw1 * inverse
    nw2 = neighbours(w2)
    zs[...] = z0
    w1s[...] = w1
    w2s[...] = w2
    pairs = ((z0, resid), (z0, nz), (w1, nz), (w1, nw1), (w2, nw1), (w2, nw2))
    parts = []
    for a, b in pairs:
        prod = a[:rows, :cols] * b[:rows, :cols]
        prod = prod[:, :128] + prod[:, 128:] if cols == 256 else sum(
            prod[:, c : c + 128] for c in range(0, cols, 128))
        parts.append(jnp.sum(prod, axis=0, keepdims=True))
    parts.append(jnp.zeros((8 - len(parts), 128), F32))
    red1[lon] = jnp.concatenate(parts, axis=0)

    def exchange(ref, send, recv, me, count, device):
        copies = []
        for d in range(1, count):
            target = lax.rem(me + d, count)
            copies.append(pltpu.make_async_remote_copy(
                src_ref=ref.at[me], dst_ref=ref.at[me], send_sem=send.at[d], recv_sem=recv.at[d],
                device_id=device(target), device_id_type=MESH))
        for c in copies:
            c.start()
        return copies

    def arrived(ref, send, recv, me, count, device):
        for d in range(1, count):
            source = lax.rem(me + count - d, count)
            pltpu.make_async_remote_copy(
                src_ref=ref.at[source], dst_ref=ref.at[source], send_sem=send.at[d], recv_sem=recv.at[d],
                device_id=device(source), device_id_type=MESH).wait_recv()

    along_lon = (red1, send1, recv1, lon, nlon, lambda t: (t, lat))
    along_lat = (red2, send2, recv2, lat, nlat, lambda t: (lon, t))
    copies1 = exchange(*along_lon)
    pl.loop(cut1, cut2)(network)
    arrived(*along_lon)
    red2[lat] = jnp.sum(red1[...], axis=0)
    copies2 = exchange(*along_lat)
    pl.loop(cut2, groups)(network)

    col_id = lax.broadcasted_iota(jnp.int32, (rows, cols), 1)
    line_id = lax.broadcasted_iota(jnp.int32, (rows, cols), 0)
    for l in range(lev):
        def around(ref, m):
            a = ref[l]
            to = HALO * 4 + m * lev + l
            at = 32 + m * lev + l
            e = jnp.where(col_id == cols - 1, recv_e[:rows, to : to + 1], shift_to(a, 1, 1))
            w = jnp.where(col_id == 0, recv_w[:rows, to : to + 1], shift_to(a, -1, 1))
            n = jnp.where(line_id == rows - 1, recv_n[at : at + 1, :] * open_n, shift_to(a, 1, 0))
            s = jnp.where(line_id == 0, recv_s[at : at + 1, :] * open_s, shift_to(a, -1, 0))
            return e, w, n, s

        e, w, n, s = around(msk_s, 0)
        we, ww, wn, ws = around(wet_s, 1)
        t = tr[l]
        lap = (e + w + n + s) - t * (we + ww + wn + ws)
        adv = -0.5 * (uu[l] * (e - w) + vv[l] * (n - s))
        tr_out[l] = t + 0.2 * wet_s[l] * (lap + adv + clo_s[l])

    arrived(*along_lat)
    total = jnp.sum(jnp.sum(red2[...], axis=0), axis=1, keepdims=True)
    moments = [total[k : k + 1, :] for k in range(6)]
    c = cg_coefficients(moments, 3, 1.0 + 4.0 * lev + 1.0)
    x = X[...] + c[0] * zs[...] + c[1] * w1s[...] + c[2] * w2s[...]
    s_out[...] = x[:rows, :cols]
    half_x = 0.5 * (shift_to(x, 1, 1) - shift_to(x, -1, 1))[:rows, :cols]
    half_y = 0.5 * (shift_to(x, 1, 0) - shift_to(x, -1, 0))[:rows, :cols]
    zs[:rows, :cols] = half_x
    w1s[:rows, :cols] = half_y

    @pl.loop(0, rows // step)
    def _(g):
        rs = pl.ds(pl.multiple_of(g * step, step), step)
        gx, gy = zs[rs, :cols], w1s[rs, :cols]
        for l in range(lev):
            wet = wet_s[l, rs, :]
            u_out[l, rs, :] = wet * (u_out[l, rs, :] - gx)
            v_out[l, rs, :] = wet * (v_out[l, rs, :] - gy)

    for c in halo_copies + copies1 + copies2:
        c.wait_send()


def on_device(nlon, nlat, tracer, u_vel, v_vel, surface, land_mask, bottom, w_in, b_in, w_mid, b_mid, w_out):
    lev, rows, cols = tracer.shape
    hid = w_mid.shape[0]
    ext = (rows + 16, cols + 128)
    cube = jax.ShapeDtypeStruct(tracer.shape, F32)
    vmem = pl.BlockSpec(memory_space=pltpu.VMEM)
    strip = 32 + 2 * lev
    scratch = (
        [pltpu.VMEM(tracer.shape, F32)] * 3
        + [pltpu.VMEM(ext, F32)] * 7
        + [
            pltpu.VMEM((8 * hid, 24 * lev), BF16),
            pltpu.VMEM((hid, hid), BF16),
            pltpu.VMEM((8 * lev, 8 * hid), BF16),
            pltpu.VMEM((hid, cols), F32),
            pltpu.VMEM((hid, cols), F32),
            pltpu.VMEM((8 * hid, cols), BF16),
            pltpu.VMEM((8 * hid, cols), BF16),
        ]
        + [pltpu.VMEM((rows, 128), F32)] * 2
        + [pltpu.VMEM((strip, cols), F32)] * 2
        + [pltpu.VMEM((rows + 16, 128), F32)] * 2
        + [pltpu.VMEM((strip, cols), F32)] * 2
        + [pltpu.VMEM((nlon, 8, 128), F32), pltpu.VMEM((nlat, 8, 128), F32)]
        + [pltpu.SemaphoreType.DMA((8,))] * 2
        + [pltpu.SemaphoreType.DMA((nlon,))] * 2
        + [pltpu.SemaphoreType.DMA((nlat,))] * 2
    )
    return pl.pallas_call(
        functools.partial(kernel, nlon, nlat),
        out_shape=(cube, cube, cube, jax.ShapeDtypeStruct(surface.shape, F32)),
        in_specs=[vmem] * 11,
        out_specs=(vmem,) * 4,
        scratch_shapes=scratch,
        compiler_params=pltpu.CompilerParams(
            collective_id=0, has_side_effects=True, vmem_limit_bytes=48 * 2**20),
    )(tracer, u_vel, v_vel, surface, land_mask, bottom, w_in, b_in[None], w_mid, b_mid[None], w_out)


def solution(mesh):
    cube, plane = P(None, "lat", "lon"), P("lat", "lon")
    return jax.shard_map(
        functools.partial(on_device, mesh.shape["lon"], mesh.shape["lat"]),
        mesh=mesh,
        in_specs=(cube, cube, cube, plane, cube, plane, P(), P(), P(), P(), P()),
        out_specs=(cube, cube, cube, plane),
        check_vma=False,
    )
```

time: 329 us -> 34.3 us (0.10)
  blocking collectives: 196 us -> 0 us
  other arithmetic: 40.8 us -> 0 us
  starting transfers between devices: 37.7 us -> 0 us
  Pallas kernels: 0 us -> 23.4 us
  waiting for transfers between devices: 17.1 us -> 0 us
  matrix products: 13 us -> 0 us
  between operations: 7.62 us -> 0.67 us
  local copies, waits for them, and re-layouts: 14.7 us -> 9.85 us
    psum x5 -> x0, blocking collectives: 196 us -> none  [total(): return lax.psum(value, ('lon', 'lat'))]
    ppermute x24 -> x0, starting transfers between devices: 37.7 us -> none  [the longest x12 25.8 us: extended(): lax.ppermute(lax.slice_in_dim(block, 0, width, axis=dim), axis, backward)]
    pallas_call x0 -> x1, Pallas kernels: none -> 23.4 us  [on_device(): pl.pallas_call(functools.partial(kernel, nlon, nlat), out_shape=(cube, cu...]
    ppermute x24 -> x0, waiting for transfers between devices: 17.1 us -> none  [the longest x12 12.5 us: extended(): lax.ppermute(lax.slice_in_dim(block, block.shape[dim] - width, None, axis...]
    reduce_sum x6 -> x0, other arithmetic: 13.3 us -> none  [the longest x3 5.78 us: solve(): alpha = rz / total(jnp.sum(p * q))]
    dot_general x2 -> x0, matrix products: 13 us -> none  [the longest x1 7.9 us: on_device(): jnp.dot(w_out.T, hidden_two, preferred_element_type=jnp.float32)]
    add x4 -> x0, other arithmetic: 10.8 us -> none  [the longest x1 9.66 us: on_device(): tracer_new = tracer + 0.2 * wet * (lap + adv + closure)]
    slice x8 -> x0, local copies, waits for them, and re-layouts: 8.43 us -> none  [the longest x7 6.02 us: extended(): lax.slice_in_dim(block, block.shape[dim] - width, None, axis=dim)]
  transfers between devices with their start and end apart: 24 -> 0, of which waited for: 11 -> 0; matrix products, arithmetic and copies ran while one was open for 12% -> 0% of each run, Pallas kernels for 0% -> 0%
where the time goes in v1:
time: 34.3 us; the launch traced here: 33.9 us
  Pallas kernels  23.4 us (68%)
  local copies, waits for them, and re-layouts  9.85 us (29%)
  between operations  0.67 us (2%)
    pallas_call x1, Pallas kernels, on_device(): pl.pallas_call(functools.partial(kernel, nlon, nlat), out_shape=(cube, cu...  23.4 us
    unnamed x23, local copies, waits for them, and re-layouts  9.85 us

profile of v1, /device:TPU:0, one launch (start us, length us, event | category | flops | bytes accessed | tf_op | source)
XLA Modules:
  0.0 33.9 jit_solution(11994971983414224302)
XLA Ops:
  0.6 0.0 copy-start.8
  0.6 0.0 copy-start.4
  0.7 0.7 %copy-done.8 = bf16[128,8]{0,1:T(8,128)(2,1)S(1)} copy-done((bf16[128,8]{0,1:T(8,128)(2,1)S(1)}, bf16[128,8]{0,1:T(8,128)(2,1)}, u32[]{:S(2)}) %copy-start.8) | copy-done | bytes 2072
  1.3 0.0 copy-start.6
  1.3 0.0 copy-start.7
  1.3 0.1 copy.15.w_out
  1.4 0.0 copy-done.4
  1.4 0.5 %copy-done.6 = f32[128]{0:T(128)S(1)} copy-done((f32[128]{0:T(128)S(1)}, f32[128]{0:T(128)}, u32[]{:S(2)}) %copy-start.6) | copy-done | bytes 536
  2.0 0.0 copy-done.7
  2.0 0.0 copy-start
  2.0 1.2 %copy-done = f32[8,128,256]{2,1,0:T(8,128)S(1)} copy-done((f32[8,128,256]{2,1,0:T(8,128)S(1)}, f32[8,128,256]{2,1,0:T(8,128)}, u32[]{:S(2)}) %copy-start) | copy-done | bytes 1048600
  3.2 0.0 copy-start.1
  3.2 1.2 %copy-done.1 = f32[8,128,256]{2,1,0:T(8,128)S(1)} copy-done((f32[8,128,256]{2,1,0:T(8,128)S(1)}, f32[8,128,256]{2,1,0:T(8,128)}, u32[]{:S(2)}) %copy-start.1) | copy-done | bytes 1048600
  4.4 0.0 copy-start.2
  4.4 0.9 %copy-done.2 = f32[128,256]{1,0:T(8,128)S(1)} copy-done((f32[128,256]{1,0:T(8,128)S(1)}, f32[128,256]{1,0:T(8,128)}, u32[]{:S(2)}) %copy-start.2) | copy-done | bytes 131096
  5.3 0.0 copy-start.3
  5.3 0.9 %copy-done.3 = s32[128,256]{1,0:T(8,128)S(1)} copy-done((s32[128,256]{1,0:T(8,128)S(1)}, s32[128,256]{1,0:T(8,128)}, u32[]{:S(2)}) %copy-start.3) | copy-done | bytes 131096
  6.2 0.0 copy-start.5
  6.3 0.7 %copy-done.5 = bf16[24,128]{1,0:T(8,128)(2,1)S(1)} copy-done((bf16[24,128]{1,0:T(8,128)(2,1)S(1)}, bf16[24,128]{1,0:T(8,128)(2,1)}, u32[]{:S(2)}) %copy-start.5) | copy-done | bytes 6168
  6.9 23.4 %shard_map.138 = (f32[8,128,256]{2,1,0:T(8,128)S(1)}, f32[8,128,256]{2,1,0:T(8,128)S(1)}, f32[8,128,256]{2,1,0:T(8,128)S(1)}, f32[128,256]{1,0:T(8,128)S(1)}) custom-call(f32[8,128,256]{2,1,0:T(8,128)S(1)} %copy-done, f32[8,128,256]{2,1,0:T(8,128)S(1)} %copy-done.1, f32[8,128,256]{2,1,0:T(8,128)} %vv.1, f32[128,256]{1,0:T(8,128)S(1)} %copy-done.2, ...), custom_call_target="tpu_custom_call" | custom-call | tf_op jit(solution)/shard_map/pallas_call | solution.py:351
  30.3 1.0 %copy.20 = f32[8,128,256]{2,1,0:T(8,128)} copy(f32[8,128,256]{2,1,0:T(8,128)S(1)} %get-tuple-element.8) | data formatting | bytes 2097152
  31.3 1.0 %copy.21 = f32[8,128,256]{2,1,0:T(8,128)} copy(f32[8,128,256]{2,1,0:T(8,128)S(1)} %get-tuple-element.9) | data formatting | bytes 2097152
  32.3 1.0 %copy.22 = f32[8,128,256]{2,1,0:T(8,128)} copy(f32[8,128,256]{2,1,0:T(8,128)S(1)} %get-tuple-element.10) | data formatting | bytes 2097152
  33.2 0.7 %copy.23 = f32[128,256]{1,0:T(8,128)} copy(f32[128,256]{1,0:T(8,128)S(1)} %get-tuple-element.11) | data formatting | bytes 262144
Async XLA Ops:
  0.6 0.7 %copy-start.8 = (bf16[128,8]{0,1:T(8,128)(2,1)S(1)}, bf16[128,8]{0,1:T(8,128)(2,1)}, u32[]{:S(2)}) copy-start(bf16[128,8]{0,1:T(8,128)(2,1)} %param.21) | copy-start | bytes 6148
  0.6 0.8 %copy-start.4 = (bf16[128,128]{1,0:T(8,128)(2,1)S(1)}, bf16[128,128]{1,0:T(8,128)(2,1)}, u32[]{:S(2)}) copy-start(bf16[128,128]{1,0:T(8,128)(2,1)} %w_mid.1) | copy-start | bytes 98308
  1.3 0.7 %copy-start.6 = (f32[128]{0:T(128)S(1)}, f32[128]{0:T(128)}, u32[]{:S(2)}) copy-start(f32[128]{0:T(128)} %param.18) | copy-start | bytes 1540
  1.3 0.7 %copy-start.7 = (f32[128]{0:T(128)S(1)}, f32[128]{0:T(128)}, u32[]{:S(2)}) copy-start(f32[128]{0:T(128)} %param.20) | copy-start | bytes 1540
  2.0 1.2 %copy-start = (f32[8,128,256]{2,1,0:T(8,128)S(1)}, f32[8,128,256]{2,1,0:T(8,128)}, u32[]{:S(2)}) copy-start(f32[8,128,256]{2,1,0:T(8,128)} %tr.1) | copy-start | bytes 3145732
  3.2 1.2 %copy-start.1 = (f32[8,128,256]{2,1,0:T(8,128)S(1)}, f32[8,128,256]{2,1,0:T(8,128)}, u32[]{:S(2)}) copy-start(f32[8,128,256]{2,1,0:T(8,128)} %uu.1) | copy-start | bytes 3145732
  4.4 0.9 %copy-start.2 = (f32[128,256]{1,0:T(8,128)S(1)}, f32[128,256]{1,0:T(8,128)}, u32[]{:S(2)}) copy-start(f32[128,256]{1,0:T(8,128)} %surf.1) | copy-start | bytes 393220
  5.3 0.9 %copy-start.3 = (s32[128,256]{1,0:T(8,128)S(1)}, s32[128,256]{1,0:T(8,128)}, u32[]{:S(2)}) copy-start(s32[128,256]{1,0:T(8,128)} %bot.1) | copy-start | bytes 393220
  6.2 0.7 %copy-start.5 = (bf16[24,128]{1,0:T(8,128)(2,1)S(1)}, bf16[24,128]{1,0:T(8,128)(2,1)}, u32[]{:S(2)}) copy-start(bf16[24,128]{1,0:T(8,128)(2,1)} %w_in.1) | copy-start | bytes 18436

commit v2 on v1

--- a/solution.py
+++ b/solution.py
@@ -8,10 +8,10 @@
 from jax.sharding import PartitionSpec as P
 
 MESH = pl.DeviceIdType.MESH
+QUARTERS = 4
 HALO = 4
 F32 = jnp.float32
 BF16 = jnp.bfloat16
-NT = (((1,), (1,)), ((), ()))
 TN = (((0,), (0,)), ((), ()))
 
 
@@ -68,18 +68,33 @@
 
 def kernel(
     nlon, nlat,
+    tr_h, uu_h, vv_h, surf_h, land_h, bot_h, w_in_h, b_in_h, w_mid_h, b_mid_h, w_out_h,
+    tr_out, u_out, v_out, s_out, wet_s, gx_out, gy_out,
     tr, uu, vv, surf, land, bot, w_in, b_in, w_mid, b_mid, w_out,
-    tr_out, u_out, v_out, s_out,
-    wet_s, msk_s, clo_s, X, U, V, D, zs, w1s, w2s,
+    msk_s, clo_s, X, U, V, D, zs, w1s, w2s,
     wbig, wmt, wob, bias1, bias2, h1, h2,
     pack_w, pack_e, row_n, row_s, recv_e, recv_w, recv_n, recv_s,
-    red1, red2, halo_send, halo_recv, send1, recv1, send2, recv2,
+    red1, red2, load_small, load_big, halo_send, halo_recv, send1, recv1, send2, recv2,
 ):
     lev, rows, cols = tr.shape
     hid = w_mid.shape[0]
     lon, lat = lax.axis_index("lon"), lax.axis_index("lat")
     east, west = lax.rem(lon + 1, nlon), lax.rem(lon + nlon - 1, nlon)
     north, south = lax.rem(lat + 1, nlat), lax.rem(lat + nlat - 1, nlat)
+
+    small = []
+    for i, (src, dst) in enumerate((
+        (w_in_h, w_in), (w_mid_h, w_mid), (w_out_h, w_out), (b_in_h, b_in), (b_mid_h, b_mid),
+        (bot_h, bot), (surf_h, surf),
+    )):
+        small.append(pltpu.make_async_copy(src, dst, load_small.at[i]))
+    big = []
+    for q in range(QUARTERS):
+        part = pl.ds(q * (rows // QUARTERS), rows // QUARTERS)
+        for i, (src, dst) in enumerate(((land_h, land), (uu_h, uu), (vv_h, vv), (tr_h, tr))):
+            big.append(pltpu.make_async_copy(src.at[:, part], dst.at[:, part], load_big.at[4 * q + i]))
+    for c in small + big:
+        c.start()
 
     barrier = pltpu.get_barrier_semaphore()
     for d in range(1, nlon):
@@ -90,10 +105,32 @@
         for b in (north, south):
             pl.semaphore_signal(barrier, inc=1, device_id=(a, b), device_id_type=MESH)
 
+    for c in small:
+        c.wait()
+
+    nf = w_in.shape[0]
+    spread = (lax.broadcasted_iota(jnp.int32, (nf, nf * 8), 0)
+              == lax.broadcasted_iota(jnp.int32, (nf, nf * 8), 1) // 8).astype(F32).astype(BF16)
+    wide = lax.dot_general(w_in[...], spread, TN, preferred_element_type=F32)
+    which = lax.broadcasted_iota(jnp.int32, wide.shape, 1) % 8
+    for jj in range(8):
+        wbig[jj * hid : (jj + 1) * hid, :] = jnp.where(which == jj, wide, 0.0).astype(BF16)
+    eye = (lax.broadcasted_iota(jnp.int32, (hid, hid), 0)
+           == lax.broadcasted_iota(jnp.int32, (hid, hid), 1))
+    wmt[...] = lax.dot_general(w_mid[...], eye.astype(F32).astype(BF16), TN, preferred_element_type=F32).astype(BF16)
+    pick = (lax.broadcasted_iota(jnp.int32, (lev * 8, lev), 0) // 8
+            == lax.broadcasted_iota(jnp.int32, (lev * 8, lev), 1)).astype(F32).astype(BF16)
+    tall = jnp.dot(pick, w_out[...], preferred_element_type=F32)
+    which = lax.broadcasted_iota(jnp.int32, tall.shape, 0) % 8
+    for jj in range(8):
+        wob[:, jj * hid : (jj + 1) * hid] = jnp.where(which == jj, tall, 0.0).astype(BF16)
+    for b, bias in ((b_in, bias1), (b_mid, bias2)):
+        column = jnp.sum(jnp.where(eye, b[...], 0.0), axis=1, keepdims=True)
+        bias[...] = jnp.broadcast_to(column, bias.shape)
+
     step = 8
 
-    @pl.loop(0, rows // step)
-    def _(g):
+    def momentum(g):
         r0 = pl.multiple_of(g * step, step)
         rs = pl.ds(r0, step)
         bottom = bot[rs, :]
@@ -119,6 +156,12 @@
         D[rs, :cols] = sd
         X[rs, :cols] = surf[rs, :]
 
+    for q in range(QUARTERS):
+        for c in big[4 * q : 4 * q + 4]:
+            c.wait()
+        per = rows // step // QUARTERS
+        pl.loop(q * per, (q + 1) * per)(momentum)
+
     lane = lax.broadcasted_iota(jnp.int32, (rows, 128), 1)
     fields = (U, V, D, X)
     for pack, at, edge, width_at in ((pack_w, 0, 0, 0), (pack_e, cols - 128, 127, 128 - HALO)):
@@ -158,26 +201,6 @@
             device_id=dev, device_id_type=MESH))
     for c in halo_copies:
         c.start()
-
-    nf = w_in.shape[0]
-    spread = (lax.broadcasted_iota(jnp.int32, (nf, nf * 8), 0)
-              == lax.broadcasted_iota(jnp.int32, (nf, nf * 8), 1) // 8).astype(F32).astype(BF16)
-    wide = lax.dot_general(w_in[...], spread, TN, preferred_element_type=F32)
-    which = lax.broadcasted_iota(jnp.int32, wide.shape, 1) % 8
-    for jj in range(8):
-        wbig[jj * hid : (jj + 1) * hid, :] = jnp.where(which == jj, wide, 0.0).astype(BF16)
-    eye = (lax.broadcasted_iota(jnp.int32, (hid, hid), 0)
-           == lax.broadcasted_iota(jnp.int32, (hid, hid), 1))
-    wmt[...] = lax.dot_general(w_mid[...], eye.astype(F32).astype(BF16), TN, preferred_element_type=F32).astype(BF16)
-    pick = (lax.broadcasted_iota(jnp.int32, (lev * 8, lev), 0) // 8
-            == lax.broadcasted_iota(jnp.int32, (lev * 8, lev), 1)).astype(F32).astype(BF16)
-    tall = lax.dot_general(pick, w_out[...], NT, preferred_element_type=F32)
-    which = lax.broadcasted_iota(jnp.int32, tall.shape, 0) % 8
-    for jj in range(8):
-        wob[:, jj * hid : (jj + 1) * hid] = jnp.where(which == jj, tall, 0.0).astype(BF16)
-    for b, bias in ((b_in, bias1), (b_mid, bias2)):
-        column = jnp.sum(jnp.where(eye, b[...], 0.0), axis=1, keepdims=True)
-        bias[...] = jnp.broadcast_to(column, bias.shape)
 
     def network(g):
         rs = pl.ds(pl.multiple_of(g * 8, 8), 8)
@@ -302,22 +325,40 @@
     c = cg_coefficients(moments, 3, 1.0 + 4.0 * lev + 1.0)
     x = X[...] + c[0] * zs[...] + c[1] * w1s[...] + c[2] * w2s[...]
     s_out[...] = x[:rows, :cols]
-    half_x = 0.5 * (shift_to(x, 1, 1) - shift_to(x, -1, 1))[:rows, :cols]
-    half_y = 0.5 * (shift_to(x, 1, 0) - shift_to(x, -1, 0))[:rows, :cols]
-    zs[:rows, :cols] = half_x
-    w1s[:rows, :cols] = half_y
-
-    @pl.loop(0, rows // step)
-    def _(g):
-        rs = pl.ds(pl.multiple_of(g * step, step), step)
-        gx, gy = zs[rs, :cols], w1s[rs, :cols]
-        for l in range(lev):
-            wet = wet_s[l, rs, :]
-            u_out[l, rs, :] = wet * (u_out[l, rs, :] - gx)
-            v_out[l, rs, :] = wet * (v_out[l, rs, :] - gy)
+    gx_out[...] = 0.5 * (shift_to(x, 1, 1) - shift_to(x, -1, 1))[:rows, :cols]
+    gy_out[...] = 0.5 * (shift_to(x, 1, 0) - shift_to(x, -1, 0))[:rows, :cols]
 
     for c in halo_copies + copies1 + copies2:
         c.wait_send()
+
+
+def finish(tr, us, vs, surf, wet, gx, gy, tr_h, u_h, v_h, s_h, u, v, whole_sem, part_sem):
+    lev, rows, cols = wet.shape
+    copies = [
+        pltpu.make_async_copy(tr, tr_h, whole_sem.at[0]),
+        pltpu.make_async_copy(surf, s_h, whole_sem.at[1]),
+    ]
+    for c in copies:
+        c.start()
+    per = rows // QUARTERS
+    for q in range(QUARTERS):
+
+        @pl.loop(0, per // 8)
+        def _(g):
+            rs = pl.ds(pl.multiple_of(q * per + g * 8, 8), 8)
+            x, y = gx[rs, :], gy[rs, :]
+            for l in range(lev):
+                w = wet[l, rs, :]
+                u[l, rs, :] = w * (us[l, rs, :] - x)
+                v[l, rs, :] = w * (vs[l, rs, :] - y)
+
+        part = pl.ds(q * per, per)
+        for i, (src, dst) in enumerate(((u, u_h), (v, v_h))):
+            c = pltpu.make_async_copy(src.at[:, part], dst.at[:, part], part_sem.at[2 * q + i])
+            c.start()
+            copies.append(c)
+    for c in copies:
+        c.wait()
 
 
 def on_device(nlon, nlat, tracer, u_vel, v_vel, surface, land_mask, bottom, w_in, b_in, w_mid, b_mid, w_out):
@@ -326,9 +367,13 @@
     ext = (rows + 16, cols + 128)
     cube = jax.ShapeDtypeStruct(tracer.shape, F32)
     vmem = pl.BlockSpec(memory_space=pltpu.VMEM)
+    args = (tracer, u_vel, v_vel, surface, land_mask, bottom, w_in, b_in[None], w_mid, b_mid[None], w_out.T)
+    plane = jax.ShapeDtypeStruct(surface.shape, F32)
+    hbm = pl.BlockSpec(memory_space=pltpu.HBM)
     strip = 32 + 2 * lev
     scratch = (
-        [pltpu.VMEM(tracer.shape, F32)] * 3
+        [pltpu.VMEM(a.shape, a.dtype) for a in args]
+        + [pltpu.VMEM(tracer.shape, F32)] * 2
         + [pltpu.VMEM(ext, F32)] * 7
         + [
             pltpu.VMEM((8 * hid, 24 * lev), BF16),
@@ -344,19 +389,29 @@
         + [pltpu.VMEM((rows + 16, 128), F32)] * 2
         + [pltpu.VMEM((strip, cols), F32)] * 2
         + [pltpu.VMEM((nlon, 8, 128), F32), pltpu.VMEM((nlat, 8, 128), F32)]
+        + [pltpu.SemaphoreType.DMA((7,)), pltpu.SemaphoreType.DMA((4 * QUARTERS,))]
         + [pltpu.SemaphoreType.DMA((8,))] * 2
         + [pltpu.SemaphoreType.DMA((nlon,))] * 2
         + [pltpu.SemaphoreType.DMA((nlat,))] * 2
     )
-    return pl.pallas_call(
+    held = pl.pallas_call(
         functools.partial(kernel, nlon, nlat),
-        out_shape=(cube, cube, cube, jax.ShapeDtypeStruct(surface.shape, F32)),
-        in_specs=[vmem] * 11,
-        out_specs=(vmem,) * 4,
+        out_shape=(cube, cube, cube, plane, cube, plane, plane),
+        in_specs=[hbm] * 11,
+        out_specs=(vmem,) * 7,
         scratch_shapes=scratch,
         compiler_params=pltpu.CompilerParams(
-            collective_id=0, has_side_effects=True, vmem_limit_bytes=48 * 2**20),
-    )(tracer, u_vel, v_vel, surface, land_mask, bottom, w_in, b_in[None], w_mid, b_mid[None], w_out)
+            collective_id=0, has_side_effects=True, vmem_limit_bytes=40 * 2**20),
+    )(*[pltpu.with_memory_space_constraint(a, pltpu.HBM) for a in args])
+    return pl.pallas_call(
+        finish,
+        out_shape=(cube, cube, cube, plane),
+        in_specs=[vmem] * 7,
+        out_specs=(hbm,) * 4,
+        scratch_shapes=[pltpu.VMEM(tracer.shape, F32)] * 2
+        + [pltpu.SemaphoreType.DMA((2,)), pltpu.SemaphoreType.DMA((2 * QUARTERS,))],
+        compiler_params=pltpu.CompilerParams(vmem_limit_bytes=40 * 2**20),
+    )(*held)
 
 
 def solution(mesh):

time: 34.3 us -> 26.4 us (0.77)
  local copies, waits for them, and re-layouts: 9.85 us -> 0 us
  Pallas kernels: 23.4 us -> 25.6 us
    unnamed x23 -> x0, local copies, waits for them, and re-layouts: 9.85 us -> none
    pallas_call x0 -> x1, Pallas kernels: none -> 1.78 us  [on_device(): pl.pallas_call(finish, out_shape=(cube, cube, cube, plane), in_specs=[vme...]
    pallas_call x1, Pallas kernels: 23.4 us -> 23.8 us  [on_device(): pl.pallas_call(functools.partial(kernel, nlon, nlat), out_shape=(cube, cu...]
where the time goes in v2:
time: 26.4 us; the launch traced here: 26.3 us
  Pallas kernels  25.6 us (97%)
  between operations  0.64 us (2%)
    pallas_call x1, Pallas kernels, on_device(): pl.pallas_call(functools.partial(kernel, nlon, nlat), out_shape=(cube, cu...  23.8 us
    pallas_call x1, Pallas kernels, on_device(): pl.pallas_call(finish, out_shape=(cube, cube, cube, plane), in_specs=[vme...  1.78 us

profile of v2, /device:TPU:0, one launch (start us, length us, event | category | flops | bytes accessed | tf_op | source)
XLA Modules:
  0.0 26.3 jit_solution(7725137953181298629)
XLA Ops:
  0.6 23.8 %shard_map.138 = (f32[8,128,256]{2,1,0:T(8,128)S(1)}, f32[8,128,256]{2,1,0:T(8,128)S(1)}, f32[8,128,256]{2,1,0:T(8,128)S(1)}, f32[128,256]{1,0:T(8,128)S(1)}, f3...) custom-call(f32[8,128,256]{2,1,0:T(8,128)} %tr_h.1, f32[8,128,256]{2,1,0:T(8,128)} %uu_h.1, ...), custom_call_target="tpu_custom_call" | custom-call | tf_op jit(solution)/shard_map/pallas_call | solution.py:397
  24.5 1.8 %shard_map.139 = (f32[8,128,256]{2,1,0:T(8,128)}, f32[8,128,256]{2,1,0:T(8,128)}, f32[8,128,256]{2,1,0:T(8,128)}, f32[128,256]{1,0:T(8,128)}) custom-call(f32[8,128,256]{2,1,0:T(8,128)S(1)} %get-tuple-element.11.tr, f32[8,128,256]{2,1,0:T(8,128)S(1)} %get-tuple-element.12.us, f32[8,128,256]{2,1,0:T(8,128)S(1)} %get-tuple-element.13.vs, ...), custom_call_target="tpu_custom_call" | custom-call | tf_op jit(solution)/shard_map/pallas_call | solution.py:406

commit v3 on v2

--- a/solution.py
+++ b/solution.py
@@ -74,7 +74,7 @@
     msk_s, clo_s, X, U, V, D, zs, w1s, w2s,
     wbig, wmt, wob, bias1, bias2, h1, h2,
     pack_w, pack_e, row_n, row_s, recv_e, recv_w, recv_n, recv_s,
-    red1, red2, load_small, load_big, halo_send, halo_recv, send1, recv1, send2, recv2,
+    red1, load_small, load_big, halo_send, halo_recv, send1, recv1,
 ):
     lev, rows, cols = tr.shape
     hid = w_mid.shape[0]
@@ -97,13 +97,10 @@
         c.start()
 
     barrier = pltpu.get_barrier_semaphore()
-    for d in range(1, nlon):
-        pl.semaphore_signal(barrier, inc=1, device_id=(lax.rem(lon + d, nlon), lat), device_id_type=MESH)
-    for d in range(1, nlat):
-        pl.semaphore_signal(barrier, inc=1, device_id=(lon, lax.rem(lat + d, nlat)), device_id_type=MESH)
-    for a in (east, west):
-        for b in (north, south):
-            pl.semaphore_signal(barrier, inc=1, device_id=(a, b), device_id_type=MESH)
+    me, count = lon * nlat + lat, nlon * nlat
+    for d in range(1, count):
+        t = lax.rem(me + d, count)
+        pl.semaphore_signal(barrier, inc=1, device_id=(t // nlat, lax.rem(t, nlat)), device_id_type=MESH)
 
     for c in small:
         c.wait()
@@ -182,7 +179,7 @@
             buf[32 + l : 33 + l, :] = msk_s[l, edge : edge + 1, :]
             buf[32 + lev + l : 33 + lev + l, :] = wet_s[l, edge : edge + 1, :]
 
-    pl.semaphore_wait(barrier, nlon - 1 + nlat - 1 + 4)
+    pl.semaphore_wait(barrier, count - 1)
 
     plan = (
         (pack_w, recv_e.at[pl.ds(0, rows)], (west, lat)),
@@ -199,8 +196,30 @@
         halo_copies.append(pltpu.make_async_remote_copy(
             src_ref=src, dst_ref=dst, send_sem=halo_send.at[i], recv_sem=halo_recv.at[i],
             device_id=dev, device_id_type=MESH))
-    for c in halo_copies:
-        c.start()
+    has_north, has_south = lat < nlat - 1, lat > 0
+    sent_if = (None, None, has_north, has_south, has_north, has_north, has_south, has_south)
+    come_if = (None, None, has_south, has_north, has_south, has_south, has_north, has_north)
+
+    def each(conditions, act):
+        for c, condition in zip(halo_copies, conditions):
+            if condition is None:
+                act(c)
+            else:
+                pl.when(condition)(functools.partial(act, c))
+
+    each(sent_if, lambda c: c.start())
+
+    @pl.when(lat == nlat - 1)
+    def _():
+        recv_n[...] = jnp.zeros_like(recv_n)
+        for ref in (recv_e, recv_w):
+            ref[rows : rows + 8, :] = jnp.zeros((8, 128), F32)
+
+    @pl.when(lat == 0)
+    def _():
+        recv_s[...] = jnp.zeros_like(recv_s)
+        for ref in (recv_e, recv_w):
+            ref[rows + 8 :, :] = jnp.zeros((8, 128), F32)
 
     def network(g):
         rs = pl.ds(pl.multiple_of(g * 8, 8), 8)
@@ -218,11 +237,10 @@
         clo_s[:, rs, :] = out.reshape(lev, 8, cols)
 
     groups = rows // 8
-    cut1, cut2 = groups // 2, groups * 3 // 4
-    pl.loop(0, cut1)(network)
-
-    for c in halo_copies:
-        c.wait_recv()
+    cut1 = groups // 2
+    pl.loop(0, cut1, unroll=4)(network)
+
+    each(come_if, lambda c: c.wait_recv())
 
     open_n = jnp.where(lat == nlat - 1, 0.0, 1.0).astype(F32)
     open_s = jnp.where(lat == 0, 0.0, 1.0).astype(F32)
@@ -270,7 +288,7 @@
             prod[:, c : c + 128] for c in range(0, cols, 128))
         parts.append(jnp.sum(prod, axis=0, keepdims=True))
     parts.append(jnp.zeros((8 - len(parts), 128), F32))
-    red1[lon] = jnp.concatenate(parts, axis=0)
+    red1[me] = jnp.concatenate(parts, axis=0)
 
     def exchange(ref, send, recv, me, count, device):
         copies = []
@@ -290,14 +308,9 @@
                 src_ref=ref.at[source], dst_ref=ref.at[source], send_sem=send.at[d], recv_sem=recv.at[d],
                 device_id=device(source), device_id_type=MESH).wait_recv()
 
-    along_lon = (red1, send1, recv1, lon, nlon, lambda t: (t, lat))
-    along_lat = (red2, send2, recv2, lat, nlat, lambda t: (lon, t))
-    copies1 = exchange(*along_lon)
-    pl.loop(cut1, cut2)(network)
-    arrived(*along_lon)
-    red2[lat] = jnp.sum(red1[...], axis=0)
-    copies2 = exchange(*along_lat)
-    pl.loop(cut2, groups)(network)
+    everyone = (red1, send1, recv1, me, count, lambda t: (t // nlat, lax.rem(t, nlat)))
+    copies1 = exchange(*everyone)
+    pl.loop(cut1, groups, unroll=4)(network)
 
     col_id = lax.broadcasted_iota(jnp.int32, (rows, cols), 1)
     line_id = lax.broadcasted_iota(jnp.int32, (rows, cols), 0)
@@ -319,8 +332,8 @@
         adv = -0.5 * (uu[l] * (e - w) + vv[l] * (n - s))
         tr_out[l] = t + 0.2 * wet_s[l] * (lap + adv + clo_s[l])
 
-    arrived(*along_lat)
-    total = jnp.sum(jnp.sum(red2[...], axis=0), axis=1, keepdims=True)
+    arrived(*everyone)
+    total = jnp.sum(jnp.sum(red1[...], axis=0), axis=1, keepdims=True)
     moments = [total[k : k + 1, :] for k in range(6)]
     c = cg_coefficients(moments, 3, 1.0 + 4.0 * lev + 1.0)
     x = X[...] + c[0] * zs[...] + c[1] * w1s[...] + c[2] * w2s[...]
@@ -328,7 +341,8 @@
     gx_out[...] = 0.5 * (shift_to(x, 1, 1) - shift_to(x, -1, 1))[:rows, :cols]
     gy_out[...] = 0.5 * (shift_to(x, 1, 0) - shift_to(x, -1, 0))[:rows, :cols]
 
-    for c in halo_copies + copies1 + copies2:
+    each(sent_if, lambda c: c.wait_send())
+    for c in copies1:
         c.wait_send()
 
 
@@ -388,11 +402,10 @@
         + [pltpu.VMEM((strip, cols), F32)] * 2
         + [pltpu.VMEM((rows + 16, 128), F32)] * 2
         + [pltpu.VMEM((strip, cols), F32)] * 2
-        + [pltpu.VMEM((nlon, 8, 128), F32), pltpu.VMEM((nlat, 8, 128), F32)]
+        + [pltpu.VMEM((nlon * nlat, 8, 128), F32)]
         + [pltpu.SemaphoreType.DMA((7,)), pltpu.SemaphoreType.DMA((4 * QUARTERS,))]
         + [pltpu.SemaphoreType.DMA((8,))] * 2
-        + [pltpu.SemaphoreType.DMA((nlon,))] * 2
-        + [pltpu.SemaphoreType.DMA((nlat,))] * 2
+        + [pltpu.SemaphoreType.DMA((nlon * nlat,))] * 2
     )
     held = pl.pallas_call(
         functools.partial(kernel, nlon, nlat),

time: 26.4 us -> 23.6 us (0.89)
  Pallas kernels: 25.6 us -> 22.8 us
    pallas_call x1, Pallas kernels: 23.8 us -> 21 us  [on_device(): pl.pallas_call(functools.partial(kernel, nlon, nlat), out_shape=(cube, cu...]
where the time goes in v3:
time: 23.6 us; the launch traced here: 23.4 us
  Pallas kernels  22.8 us (97%)
  between operations  0.64 us (3%)
    pallas_call x1, Pallas kernels, on_device(): pl.pallas_call(functools.partial(kernel, nlon, nlat), out_shape=(cube, cu...  21 us
    pallas_call x1, Pallas kernels, on_device(): pl.pallas_call(finish, out_shape=(cube, cube, cube, plane), in_specs=[vme...  1.78 us

profile of v3, /device:TPU:0, one launch (start us, length us, event | category | flops | bytes accessed | tf_op | source)
XLA Modules:
  0.0 23.4 jit_solution(11122755093945320368)
XLA Ops:
  0.6 21.0 %shard_map.138 = (f32[8,128,256]{2,1,0:T(8,128)S(1)}, f32[8,128,256]{2,1,0:T(8,128)S(1)}, f32[8,128,256]{2,1,0:T(8,128)S(1)}, f32[128,256]{1,0:T(8,128)S(1)}, f3...) custom-call(f32[8,128,256]{2,1,0:T(8,128)} %tr_h.1, f32[8,128,256]{2,1,0:T(8,128)} %uu_h.1, ...), custom_call_target="tpu_custom_call" | custom-call | tf_op jit(solution)/shard_map/pallas_call | solution.py:410
  21.7 1.8 %shard_map.139 = (f32[8,128,256]{2,1,0:T(8,128)}, f32[8,128,256]{2,1,0:T(8,128)}, f32[8,128,256]{2,1,0:T(8,128)}, f32[128,256]{1,0:T(8,128)}) custom-call(f32[8,128,256]{2,1,0:T(8,128)S(1)} %get-tuple-element.11.tr, f32[8,128,256]{2,1,0:T(8,128)S(1)} %get-tuple-element.12.us, f32[8,128,256]{2,1,0:T(8,128)S(1)} %get-tuple-element.13.vs, ...), custom_call_target="tpu_custom_call" | custom-call | tf_op jit(solution)/shard_map/pallas_call | solution.py:419
